TPU v7x, 256 devices: a whole 4x4x8 slice. The times are simulated.
256 devices in a mesh: gx: 4 (over y), gy: 8 (over z), gz: 8 (over x, core).
Axes of the slice: x: 4, y: 4, z: 8, core: 2. Of those that a mesh axis runs over, the one named last changes fastest.
Arguments:
- previous: float32 [16, 32, 128, 1024], P(None, 'gx', 'gy', 'gz'), may hold values from -6 to 6
- current: float32 [16, 32, 128, 1024], P(None, 'gx', 'gy', 'gz'), may hold values from -6 to 6
- potential: float32 [32, 128, 1024], P('gx', 'gy', 'gz'), may hold values from -1 to 1
- projector: float32 [4, 8, 8, 27, 4, 18, 128], P('gx', 'gy', 'gz'), may hold values from -0.3 to 0.3
- node_index: int32 [4, 8, 8, 27, 4, 128], P('gx', 'gy', 'gz'), may hold values from 0 to 16383
- coupling: float32 [1024, 18, 18], P(('gx', 'gy', 'gz')), may hold values from -1.5 to 1.5
- cut_low: float32 [1], replicated, may hold values from 0.5 to 1.5
- cut_high: float32 [1], replicated, may hold values from 8 to 10
Outputs:
- next_field: float32 [16, 32, 128, 1024], P(None, 'gx', 'gy', 'gz')
- last_field: float32 [16, 32, 128, 1024], P(None, 'gx', 'gy', 'gz')
Inputs may be any that keep to these rules, and one draw needn't show every extreme that they name: `node_index`: local node numbers of a device's block, x slowest and z fastest.
All inputs are finite; a program needn't handle non-finite values.
Results may differ from a plain program's by a relative error of at most 0.00005.
Values sent between devices are 32-bit elements; how exact they have to be, the bound alone decides.
A program may use at most 128 MiB of HBM per device.

v0:
```python
import jax
import jax.numpy as jnp
from jax import lax
from jax.experimental import pallas as pl
from jax.experimental.pallas import tpu as pltpu
from jax.sharding import PartitionSpec as P

F32 = jnp.float32
BF16 = jnp.bfloat16
MESH = pl.DeviceIdType.MESH

BANDS = 16
ROWS = 128
LANES = 128
LINE = 16
PLANES = 8
NOFF = 27
ATOMS = 4
SHARE = 2
NPROJ = 18
PPAD = 32
PSEND = 24
HALF = ROWS // 2
CENTRE = NOFF // 2
TRIO = 3
NCHUNK = NOFF // TRIO
BLOCKS = TRIO * SHARE
WIDE = BLOCKS * LANES
DEEP = BLOCKS * PPAD
GROUP = SHARE * BANDS
OTHERS = [offset for offset in range(NOFF) if offset != CENTRE]


def split(value):
    high = value.astype(BF16)
    return high, (value - high.astype(F32)).astype(BF16)


def kernel(
    sizes,
    low_s, high_s,
    previous, current, potential, projector, index_v, coupling,
    following, last,
    onehot, proj_hi, proj_lo, halved, held, spreads, coup,
    send_c, recv_c, send_w, recv_w,
    face_y, face_z, halo_x, halo_y, halo_z,
    sem_sc, sem_rc, sem_sw, sem_rw, sem_sh, sem_rh,
):
    place = tuple(lax.axis_index(axis) for axis in ("gx", "gy", "gz"))
    centre = 0.5 * (high_s[0] + low_s[0])
    radius = 0.5 * (high_s[0] - low_s[0])
    scale = 2.0 / radius

    around = [
        (lax.rem(at + count - 1, count), at, lax.rem(at + 1, count))
        for at, count in zip(place, sizes)
    ]
    exists = [(at > 0, None, at < count - 1) for at, count in zip(place, sizes)]

    def shift_of(offset):
        return offset // 9 - 1, (offset // 3) % 3 - 1, offset % 3 - 1

    def towards(offset, sign):
        return tuple(
            around[axis][sign * step + 1] for axis, step in enumerate(shift_of(offset))
        )

    def inside(offset, sign):
        valid = None
        for axis, step in enumerate(shift_of(offset)):
            here = exists[axis][sign * step + 1]
            if here is not None:
                valid = here if valid is None else valid & here
        return valid

    barrier = pltpu.get_barrier_semaphore()

    for offset in OTHERS:
        pl.semaphore_signal(
            barrier, inc=1, device_id=towards(offset, 1), device_id_type=MESH
        )

    lane_of = lambda rows: lax.broadcasted_iota(jnp.int32, (rows, LANES), 1)
    row_of = lambda rows: lax.broadcasted_iota(jnp.int32, (rows, LANES), 0)

    def prepare(offset, carry):
        wide = lax.broadcasted_iota(jnp.int32, (2 * LANES, LANES), 0)
        for atom in range(ATOMS):
            block = (atom // SHARE * NOFF + offset) * SHARE + atom % SHARE
            values = jnp.concatenate(
                [projector[offset, :, atom, :], jnp.zeros((PPAD - NPROJ, LANES), F32)], axis=0
            )
            high, low = split(values)
            at = pl.ds(pl.multiple_of(block * PPAD, PPAD), PPAD)
            proj_hi[at, :] = high
            proj_lo[at, :] = low
            node = index_v[offset, atom:atom + 1, :]
            column = (node // (HALF * LANES)) * LANES + node % LANES
            onehot[:, pl.ds(pl.multiple_of(block * LANES, LANES), LANES)] = jnp.where(
                wide == column, 1.0, 0.0
            ).astype(BF16)
        return carry

    lax.fori_loop(0, NOFF, prepare, 0)

    coup[...] = jnp.zeros(coup.shape, F32)
    for atom in range(ATOMS):
        coup[atom * PPAD:atom * PPAD + NPROJ, 0:NPROJ] = coupling[:, atom, :]
    held[...] = jnp.zeros(held.shape, F32)
    proj_hi[ATOMS * NOFF * PPAD:, :] = jnp.zeros((SHARE * PPAD, LANES), BF16)
    proj_lo[ATOMS * NOFF * PPAD:, :] = jnp.zeros((SHARE * PPAD, LANES), BF16)

    sides = [(axis, sign) for axis in range(3) for sign in (1, -1)]

    def neighbour(axis, sign):
        return tuple(
            around[n][sign + 1] if n == axis else at for n, at in enumerate(place)
        )

    def halo_copies(step, field):
        copies = []
        for n, (axis, sign) in enumerate(sides):
            slot = 0 if sign == 1 else 1
            if axis == 0:
                source = field.at[:, pl.ds(ROWS - LINE if sign == 1 else 0, LINE), :]
                target = halo_x.at[step, slot]
            elif axis == 1:
                source, target = face_y.at[step, slot], halo_y.at[step, slot]
            else:
                source, target = face_z.at[step, slot], halo_z.at[step, slot]
            copies.append(
                pltpu.make_async_remote_copy(
                    src_ref=source, dst_ref=target,
                    send_sem=sem_sh.at[step, n], recv_sem=sem_rh.at[step, n],
                    device_id=neighbour(axis, sign), device_id_type=MESH,
                )
            )
        return copies

    def part_copy(unit, offset):
        return pltpu.make_async_remote_copy(
            src_ref=send_c.at[unit, offset], dst_ref=recv_c.at[unit, offset],
            send_sem=sem_sc.at[unit, offset], recv_sem=sem_rc.at[unit, offset],
            device_id=towards(offset, 1), device_id_type=MESH,
        )

    def weight_copy(unit, offset):
        return pltpu.make_async_remote_copy(
            src_ref=send_w.at[unit], dst_ref=recv_w.at[unit, offset],
            send_sem=sem_sw.at[unit, offset], recv_sem=sem_rw.at[unit, offset],
            device_id=towards(offset, -1), device_id_type=MESH,
        )

    third = lane_of(8) // GROUP

    def turned(value, groups):
        shift = groups * GROUP % LANES
        return pltpu.roll(value, shift, 1) if shift else value

    def row_mask(share, chunk, block):
        atom = share * SHARE + block % SHARE
        node = index_v[chunk * TRIO + block // SHARE, atom:atom + 1, :]
        return (node // LANES) % HALF == row_of(HALF)

    def contract(unit, share, chunk, slot, into):
        first = (share * NCHUNK + chunk) * DEEP
        at = pl.ds(pl.multiple_of(first, DEEP), DEEP)
        p_hi, p_lo = proj_hi[at, :], proj_lo[at, :]
        high, low = split(held[slot])
        product = lax.dot_general(
            jnp.concatenate([p_hi, p_lo, p_hi], axis=1),
            jnp.concatenate([high, high, low], axis=1),
            (((1,), (1,)), ((), ())),
            preferred_element_type=F32,
        )
        tile = jnp.zeros((PSEND, LANES), F32)
        for k in range(BLOCKS):
            tile = jnp.where(
                lane_of(PSEND) // BANDS == k, product[k * PPAD:k * PPAD + PSEND], tile
            )
        for n in range(TRIO):
            message = jnp.zeros((8, LANES), F32)
            for p in range(3):
                message = jnp.where(third == p, turned(tile[8 * p:8 * p + 8], p - n), message)
            send_c[unit, into * TRIO + n] = message

    def gather(unit, share, special, action):
        def body(chunk, carry):
            slot = lax.rem(chunk, 2)
            contract(
                unit, share, jnp.maximum(chunk - 1, 0), 1 - slot,
                lax.rem(chunk + NCHUNK, NCHUNK + 1),
            )
            for two in range(BLOCKS // 2):
                first = (share * NCHUNK + chunk) * WIDE + two * 2 * LANES
                columns = onehot[:, pl.ds(pl.multiple_of(first, 2 * LANES), 2 * LANES)]
                product = jnp.dot(
                    halved[...], jnp.concatenate([columns, columns], axis=0),
                    preferred_element_type=F32,
                )
                for n in range(2):
                    block = two * 2 + n
                    mine = product[:, n * LANES:(n + 1) * LANES].reshape(BANDS, HALF, LANES)
                    held[slot, block * BANDS:(block + 1) * BANDS, :] = jnp.sum(
                        jnp.where(row_mask(share, chunk, block)[None], mine, 0.0), axis=1
                    )
            if action is not None:
                pl.when(chunk == special)(action)
            return carry

        lax.fori_loop(0, NCHUNK, body, 0)
        contract(unit, share, NCHUNK - 1, (NCHUNK - 1) % 2, NCHUNK - 1)

    def couple(unit, share):
        total = send_c[unit, CENTRE]
        for offset in OTHERS:
            part_copy(unit, offset).wait()
            total = total + jnp.where(inside(offset, -1), recv_c[unit, offset], 0.0)
        total = jnp.concatenate(
            [turned(total, -p) for p in range(3)]
            + [jnp.zeros((LANES - PSEND, LANES), F32)], axis=0
        )
        product = jnp.dot(
            coup[share * SHARE * PPAD:(share + 1) * SHARE * PPAD, :], total, precision=lax.Precision.HIGHEST, preferred_element_type=F32
        )
        weighted = jnp.zeros((PSEND, LANES), F32)
        for atom in range(SHARE):
            weighted = jnp.where(
                lane_of(PSEND) // BANDS == atom,
                product[atom * PPAD:atom * PPAD + PSEND], weighted,
            )
        message = jnp.zeros((8, LANES), F32)
        for p in range(3):
            message = jnp.where(third == p, turned(weighted[8 * p:8 * p + 8], p), message)
        send_w[unit] = scale * message
        recv_w[unit, CENTRE] = scale * message
        for offset in OTHERS:
            weight_copy(unit, offset).start()

    def spread(unit, share, chunk, slot):
        received = [recv_w[unit, chunk * TRIO + n] for n in range(TRIO)]
        rows = []
        for p in range(3):
            row = jnp.zeros((8, LANES), F32)
            for n in range(TRIO):
                row = jnp.where(third == n, turned(received[n], n - p), row)
            rows.append(row)
        rows.append(jnp.zeros((PPAD - PSEND, LANES), F32))
        weights = jnp.concatenate(rows * (LANES // PPAD), axis=0).T
        owner = row_of(LANES) // BANDS - lane_of(LANES) // PPAD
        weights = jnp.concatenate(
            [jnp.where(owner == n * (LANES // PPAD), weights, 0.0) for n in range(2)], axis=1
        )
        high, low = split(weights)
        first = (share * NCHUNK + chunk) * DEEP
        at = pl.ds(pl.multiple_of(first, DEEP), 2 * LANES)
        p_hi, p_lo = proj_hi[at, :], proj_lo[at, :]
        spreads[slot] = jnp.dot(
            jnp.concatenate([high, low, high], axis=1),
            jnp.concatenate([p_hi, p_hi, p_lo], axis=0),
            preferred_element_type=F32,
        )

    def scatter(unit, share, result, special, action):
        def body(chunk, carry):
            high, low = split(spreads[chunk])
            parts_hi, parts_lo = [], []
            for block in range(BLOCKS):
                mask = row_mask(share, chunk, block)
                for value, parts in ((high, parts_hi), (low, parts_lo)):
                    mine = value[block * BANDS:(block + 1) * BANDS].astype(F32)
                    parts.append(
                        jnp.where(mask[None], mine[:, None, :], 0.0)
                        .astype(BF16).reshape(BANDS * HALF, LANES)
                    )
            first = (share * NCHUNK + chunk) * WIDE
            columns = onehot[:, pl.ds(pl.multiple_of(first, WIDE), WIDE)]
            product = lax.dot_general(
                jnp.concatenate(parts_hi + parts_lo, axis=1),
                jnp.concatenate([columns, columns], axis=1),
                (((1,), (1,)), ((), ())),
                preferred_element_type=F32,
            )
            product = product.reshape(BANDS, HALF, 2 * LANES)
            result[:, 0:HALF, :] += product[:, :, 0:LANES]
            result[:, HALF:ROWS, :] += product[:, :, LANES:]
            if action is not None:
                pl.when(chunk == special)(action)
            return carry

        for offset in OTHERS:
            weight_copy(unit, offset).wait()
            recv_w[unit, offset] = jnp.where(inside(offset, 1), recv_w[unit, offset], 0.0)
        def ahead(n, carry):
            for m in range(3):
                spread(unit, share, n * 3 + m, n * 3 + m)
            return carry

        lax.fori_loop(0, NCHUNK // 3, ahead, 0)
        lax.fori_loop(0, NCHUNK, body, 0, unroll=3)

    def advance(step, before, field, result):
        face_y[step, 0] = field[:, pl.ds(LINE - 1, PLANES, stride=LINE), :]
        face_y[step, 1] = field[:, pl.ds(0, PLANES, stride=LINE), :]
        top = jnp.zeros((ROWS, LANES), F32)
        bottom = jnp.zeros((ROWS, LANES), F32)
        lanes = lane_of(ROWS)
        for band in range(BANDS):
            plane = field[band]
            top = jnp.where(lanes == band, pltpu.roll(plane, band + 1, 1), top)
            bottom = jnp.where(
                lanes == band, pltpu.roll(plane, band, 1) if band else plane, bottom
            )
        face_z[step, 0] = top
        face_z[step, 1] = bottom
        def cut(band, carry):
            at = pl.ds(pl.multiple_of(band * HALF, HALF), HALF)
            high, low = split(field[band])
            for half in range(2):
                rows = slice(half * HALF, (half + 1) * HALF)
                halved[at, half * LANES:(half + 1) * LANES] = high[rows]
                halved[at, (2 + half) * LANES:(3 + half) * LANES] = low[rows]
            return carry

        lax.fori_loop(0, BANDS, cut, 0)

        first, second = 2 * step, 2 * step + 1
        halos = halo_copies(step, field)
        if step > 0:
            for copy in halos:
                copy.start()
        gather(first, 0, 0, None)
        if step == 0:
            pl.semaphore_wait(barrier, len(OTHERS))
            for copy in halos:
                copy.start()
        for offset in OTHERS:
            part_copy(first, offset).start()
        gather(second, 1, 5, lambda: couple(first, 0))
        for offset in OTHERS:
            part_copy(second, offset).start()

        for copy in halos:
            copy.wait()
        edge = [(exists[axis][0], exists[axis][2]) for axis in range(3)]
        zside = [
            jnp.where(edge[2][slot], halo_z[step, slot], 0.0) for slot in range(2)
        ]

        line_of = lax.broadcasted_iota(jnp.int32, (PLANES, LINE, LANES), 1)
        def stencil(band):
            plane = field[band]
            below_x = jnp.where(edge[0][0], halo_x[step, 0, band], 0.0)
            above_x = jnp.where(edge[0][1], halo_x[step, 1, band], 0.0)
            beside = jnp.concatenate([below_x, plane[:ROWS - LINE]], axis=0)
            beside = beside + jnp.concatenate([plane[LINE:], above_x], axis=0)
            below_y = jnp.where(edge[1][0], halo_y[step, 0, band], 0.0)
            above_y = jnp.where(edge[1][1], halo_y[step, 1, band], 0.0)
            down = pltpu.roll(plane, 1, 0).reshape(PLANES, LINE, LANES)
            up = pltpu.roll(plane, ROWS - 1, 0).reshape(PLANES, LINE, LANES)
            down = jnp.where(line_of == 0, below_y[:, None, :], down)
            up = jnp.where(line_of == LINE - 1, above_y[:, None, :], up)
            beside = beside + (down + up).reshape(ROWS, LANES)
            back = pltpu.roll(plane, 1, 1)
            ahead = pltpu.roll(plane, LANES - 1, 1)
            side_b = pltpu.roll(zside[0], (LANES - band) % LANES, 1) if band else zside[0]
            side_a = pltpu.roll(zside[1], LANES - 1 - band, 1)
            back = jnp.where(lanes == 0, side_b, back)
            ahead = jnp.where(lanes == LANES - 1, side_a, ahead)
            beside = beside + (back + ahead)
            local = 0.5 * (6.0 * plane - beside) + (potential[...] - centre) * plane
            result[band] = scale * local - before[band]

        for band in range(BANDS):
            stencil(band)

        scatter(first, 0, result, 3, lambda: couple(second, 1))
        scatter(second, 1, result, 0, None)

    advance(0, previous, current, following)
    advance(1, current, following, last)


def shards(previous, current, potential, projector, node_index, coupling, cut_low, cut_high):
    sizes = tuple(lax.axis_size(axis) for axis in ("gx", "gy", "gz"))
    shape = current.shape
    block = (BANDS, ROWS, LANES)
    vmem = pl.BlockSpec(memory_space=pltpu.VMEM)
    smem = pl.BlockSpec(memory_space=pltpu.SMEM)
    index = node_index.reshape(NOFF, ATOMS, LANES)

    def body(*refs):
        kernel(sizes, *refs)

    following, last = pl.pallas_call(
        body,
        out_shape=[jax.ShapeDtypeStruct(block, F32)] * 2,
        in_specs=[smem] * 2 + [vmem] * 6,
        out_specs=[vmem, vmem],
        scratch_shapes=[
            pltpu.VMEM((2 * LANES, NOFF * ATOMS * LANES), BF16),
            pltpu.VMEM(((NOFF * ATOMS + SHARE) * PPAD, LANES), BF16),
            pltpu.VMEM(((NOFF * ATOMS + SHARE) * PPAD, LANES), BF16),
            pltpu.VMEM((BANDS * HALF, 4 * LANES), BF16),
            pltpu.VMEM((2, LANES, LANES), F32),
            pltpu.VMEM((NCHUNK, LANES, LANES), F32),
            pltpu.VMEM((ATOMS * PPAD, LANES), F32),
            pltpu.VMEM((4, NOFF + TRIO, 8, LANES), F32),
            pltpu.VMEM((4, NOFF, 8, LANES), F32),
            pltpu.VMEM((4, 8, LANES), F32),
            pltpu.VMEM((4, NOFF, 8, LANES), F32),
            pltpu.VMEM((2, 2, BANDS, PLANES, LANES), F32),
            pltpu.VMEM((2, 2, ROWS, LANES), F32),
            pltpu.VMEM((2, 2, BANDS, LINE, LANES), F32),
            pltpu.VMEM((2, 2, BANDS, PLANES, LANES), F32),
            pltpu.VMEM((2, 2, ROWS, LANES), F32),
            pltpu.SemaphoreType.DMA((4, NOFF)),
            pltpu.SemaphoreType.DMA((4, NOFF)),
            pltpu.SemaphoreType.DMA((4, NOFF)),
            pltpu.SemaphoreType.DMA((4, NOFF)),
            pltpu.SemaphoreType.DMA((2, 6)),
            pltpu.SemaphoreType.DMA((2, 6)),
        ],
        compiler_params=pltpu.CompilerParams(
            collective_id=0, has_side_effects=True, vmem_limit_bytes=60 * 2**20
        ),
        cost_estimate=pl.CostEstimate(
            flops=60 * 10**9, bytes_accessed=8 * 2**20, transcendentals=0
        ),
    )(
        cut_low, cut_high,
        previous.reshape(block), current.reshape(block), potential.reshape(ROWS, LANES),
        jnp.swapaxes(projector.reshape(NOFF, ATOMS, NPROJ, LANES), 1, 2), index,
        jnp.swapaxes(coupling, 0, 1),
    )
    return following.reshape(shape), last.reshape(shape)


def solution(mesh):
    placed = (
        P(None, "gx", "gy", "gz"),
        P(None, "gx", "gy", "gz"),
        P("gx", "gy", "gz"),
        P("gx", "gy", "gz", None, None, None, None),
        P("gx", "gy", "gz", None, None, None),
        P(("gx", "gy", "gz"), None, None),
        P(),
        P(),
    )
    return jax.shard_map(
        shards,
        mesh=mesh,
        in_specs=placed,
        out_specs=(P(None, "gx", "gy", "gz"), P(None, "gx", "gy", "gz")),
        check_vma=False,
    )
```

profile of v0, /device:TPU:1, one launch (start us, length us, event | category | flops | bytes accessed | tf_op | source)
XLA Modules:
  0.0 108.6 jit_solution(15052960694151835692)
XLA Ops:
  1.9 103.3 %shard_map.95 = (f32[16,128,128]{2,1,0:T(8,128)}, f32[16,128,128]{2,1,0:T(8,128)}) custom-call(f32[1]{0:T(128)S(6)} %copy.12.refs_0_, f32[1]{0:T(128)S(6)} %copy.13.refs_1_, f32[16,128,128]{2,1,0:T(8,128)} %bitcast.12, f32[16,128,128]{2,1,0:T(8,128)} %bitcast.13, f32[128,128]{1,0:T(8,128)} %bitcast.15, f32[27,18,4,128]{3,2,1,0:T(4,128)} %bitcast.14, ...), custom_call_target="tpu_custom_call" | custom-call | flops 60000002048 | bytes 8388608 | tf_op jit(solution)/shard_map/pallas_call | solution.py:395
  105.2 0.0 copy-start
  105.3 2.4 %copy.14 = f32[16,8,16,128]{3,2,1,0:T(8,128)} copy(f32[16,8,16,128]{3,2,1,0:T(8,128)} %bitcast.11) | data formatting | bytes 2097152
  107.6 0.0 copy-done
  107.6 1.0 copy.15
Async XLA Ops:
  105.2 2.4 %copy-start = (f32[16,128,128]{2,1,0:T(8,128)S(1)}, f32[16,128,128]{2,1,0:T(8,128)}, u32[]{:S(2)}) copy-start(f32[16,128,128]{2,1,0:T(8,128)} %get-tuple-element.5) | copy-start | bytes 3145732
where the time goes:
time: 109 us
  Pallas kernels  103 us (94%)
  local copies, waits for them, and re-layouts  3.36 us (3%)
  between operations  1.94 us (2%)
    pallas_call x1, Pallas kernels, shards(): pl.pallas_call(body, out_shape=[jax.ShapeDtypeStruct(block, F32)] * 2, in...  103 us
    unnamed x4, local copies, waits for them, and re-layouts  3.36 us

commit v1 on v0

--- a/solution.py
+++ b/solution.py
@@ -262,19 +262,22 @@
         )
 
     def scatter(unit, share, result, special, action):
-        def body(chunk, carry):
-            high, low = split(spreads[chunk])
+        def body(turn, carry):
             parts_hi, parts_lo = [], []
-            for block in range(BLOCKS):
-                mask = row_mask(share, chunk, block)
-                for value, parts in ((high, parts_hi), (low, parts_lo)):
-                    mine = value[block * BANDS:(block + 1) * BANDS].astype(F32)
-                    parts.append(
-                        jnp.where(mask[None], mine[:, None, :], 0.0)
-                        .astype(BF16).reshape(BANDS * HALF, LANES)
-                    )
-            first = (share * NCHUNK + chunk) * WIDE
-            columns = onehot[:, pl.ds(pl.multiple_of(first, WIDE), WIDE)]
+            for m in range(3):
+                chunk = turn * 3 + m
+                high, low = split(spreads[chunk])
+                for block in range(BLOCKS):
+                    mask = row_mask(share, chunk, block)
+                    for value, parts in ((high, parts_hi), (low, parts_lo)):
+                        mine = value[block * BANDS:(block + 1) * BANDS].astype(F32)
+                        parts.append(
+                            jnp.where(mask[None], mine[:, None, :], 0.0)
+                            .astype(BF16).reshape(BANDS * HALF, LANES)
+                        )
+            width = 3 * WIDE
+            first = share * NCHUNK * WIDE + turn * width
+            columns = onehot[:, pl.ds(pl.multiple_of(first, width), width)]
             product = lax.dot_general(
                 jnp.concatenate(parts_hi + parts_lo, axis=1),
                 jnp.concatenate([columns, columns], axis=1),
@@ -285,7 +288,7 @@
             result[:, 0:HALF, :] += product[:, :, 0:LANES]
             result[:, HALF:ROWS, :] += product[:, :, LANES:]
             if action is not None:
-                pl.when(chunk == special)(action)
+                pl.when(turn == special)(action)
             return carry
 
         for offset in OTHERS:
@@ -297,7 +300,7 @@
             return carry
 
         lax.fori_loop(0, NCHUNK // 3, ahead, 0)
-        lax.fori_loop(0, NCHUNK, body, 0, unroll=3)
+        lax.fori_loop(0, NCHUNK // 3, body, 0)
 
     def advance(step, before, field, result):
         face_y[step, 0] = field[:, pl.ds(LINE - 1, PLANES, stride=LINE), :]
@@ -374,11 +377,25 @@
         for band in range(BANDS):
             stencil(band)
 
-        scatter(first, 0, result, 3, lambda: couple(second, 1))
+        scatter(first, 0, result, 1, lambda: couple(second, 1))
         scatter(second, 1, result, 0, None)
 
     advance(0, previous, current, following)
     advance(1, current, following, last)
+
+
+def hand_on(first_in, second_in, first_out, second_out, sem):
+    copies = []
+    for n, (source, target) in enumerate(((first_in, first_out), (second_in, second_out))):
+        for part in range(4):
+            bands = pl.ds(part * (BANDS // 4), BANDS // 4)
+            copies.append(
+                pltpu.make_async_copy(source.at[bands], target.at[bands], sem.at[n, part])
+            )
+    for copy in copies:
+        copy.start()
+    for copy in copies:
+        copy.wait()
 
 
 def shards(previous, current, potential, projector, node_index, coupling, cut_low, cut_high):
@@ -433,6 +450,15 @@
         jnp.swapaxes(projector.reshape(NOFF, ATOMS, NPROJ, LANES), 1, 2), index,
         jnp.swapaxes(coupling, 0, 1),
     )
+    anywhere = pl.BlockSpec(memory_space=pl.ANY)
+    following, last = pl.pallas_call(
+        hand_on,
+        out_shape=[jax.ShapeDtypeStruct(block, F32)] * 2,
+        in_specs=[anywhere] * 2,
+        out_specs=[anywhere] * 2,
+        scratch_shapes=[pltpu.SemaphoreType.DMA((2, 4))],
+        cost_estimate=pl.CostEstimate(flops=0, bytes_accessed=4 * 2**20, transcendentals=0),
+    )(following, last)
     return following.reshape(shape), last.reshape(shape)
 
 

time: 109 us -> 172 us (1.58)
  Pallas kernels: 103 us -> 169 us
  local copies, waits for them, and re-layouts: 3.36 us -> 0 us
    pallas_call x0 -> x1, Pallas kernels: none -> 64.7 us  [shards(): pl.pallas_call(hand_on, out_shape=[jax.ShapeDtypeStruct(block, F32)] * 2,...]
    unnamed x4 -> x0, local copies, waits for them, and re-layouts: 3.36 us -> none
where the time goes in v1:
time: 172 us; the launch traced here: 171 us
  Pallas kernels  169 us (98%)
  between operations  2.09 us (1%)
    pallas_call x1, Pallas kernels, shards(): pl.pallas_call(body, out_shape=[jax.ShapeDtypeStruct(block, F32)] * 2, in...  105 us
    pallas_call x1, Pallas kernels, shards(): pl.pallas_call(hand_on, out_shape=[jax.ShapeDtypeStruct(block, F32)] * 2,...  64.7 us

profile of v1, /device:TPU:1, one launch (start us, length us, event | category | flops | bytes accessed | tf_op | source)
XLA Modules:
  0.0 171.4 jit_solution(4006719892026583045)
XLA Ops:
  1.9 104.6 %shard_map.95 = (f32[16,128,128]{2,1,0:T(8,128)}, f32[16,128,128]{2,1,0:T(8,128)}) custom-call(f32[1]{0:T(128)S(6)} %copy.10.refs_0_, f32[1]{0:T(128)S(6)} %copy.11.refs_1_, f32[16,128,128]{2,1,0:T(8,128)} %bitcast.10, f32[16,128,128]{2,1,0:T(8,128)} %bitcast.11, f32[128,128]{1,0:T(8,128)} %bitcast.15, f32[27,18,4,128]{3,2,1,0:T(4,128)} %bitcast.14, ...), custom_call_target="tpu_custom_call" | custom-call | flops 60000002048 | bytes 8388608 | tf_op jit(solution)/shard_map/pallas_call | solution.py:412
  106.5 64.7 %shard_map.96 = (f32[16,128,128]{2,1,0:T(8,128)}, f32[16,128,128]{2,1,0:T(8,128)}) custom-call(f32[16,128,128]{2,1,0:T(8,128)} %get-tuple-element.6.first_in, f32[16,128,128]{2,1,0:T(8,128)} %get-tuple-element.7.second_in), custom_call_target="tpu_custom_call" | custom-call | bytes 4194304 | tf_op jit(solution)/shard_map/pallas_call | solution.py:454

commit v2 on v1

--- a/solution.py
+++ b/solution.py
@@ -384,17 +384,25 @@
     advance(1, current, following, last)
 
 
-def hand_on(first_in, second_in, first_out, second_out, sem):
-    copies = []
-    for n, (source, target) in enumerate(((first_in, first_out), (second_in, second_out))):
-        for part in range(4):
-            bands = pl.ds(part * (BANDS // 4), BANDS // 4)
-            copies.append(
-                pltpu.make_async_copy(source.at[bands], target.at[bands], sem.at[n, part])
-            )
-    for copy in copies:
+def hand_on(first_in, second_in, first_out, second_out, first_held, second_held, sem_in, sem_out):
+    coming, going = [], []
+    for part in range(4):
+        bands = pl.ds(part * (BANDS // 4), BANDS // 4)
+        for n, (source, held, target) in enumerate(
+            ((first_in, first_held, first_out), (second_in, second_held, second_out))
+        ):
+            coming.append(
+                pltpu.make_async_copy(source.at[bands], held.at[bands], sem_in.at[n, part])
+            )
+            going.append(
+                pltpu.make_async_copy(held.at[bands], target.at[bands], sem_out.at[n, part])
+            )
+    for copy in coming:
         copy.start()
-    for copy in copies:
+    for here, there in zip(coming, going):
+        here.wait()
+        there.start()
+    for copy in going:
         copy.wait()
 
 
@@ -456,7 +464,12 @@
         out_shape=[jax.ShapeDtypeStruct(block, F32)] * 2,
         in_specs=[anywhere] * 2,
         out_specs=[anywhere] * 2,
-        scratch_shapes=[pltpu.SemaphoreType.DMA((2, 4))],
+        scratch_shapes=[
+            pltpu.VMEM(block, F32),
+            pltpu.VMEM(block, F32),
+            pltpu.SemaphoreType.DMA((2, 4)),
+            pltpu.SemaphoreType.DMA((2, 4)),
+        ],
         cost_estimate=pl.CostEstimate(flops=0, bytes_accessed=4 * 2**20, transcendentals=0),
     )(following, last)
     return following.reshape(shape), last.reshape(shape)

time: 172 us -> 109 us (0.63)
  Pallas kernels: 169 us -> 107 us
    pallas_call x1, Pallas kernels: 64.7 us -> 2.39 us  [shards(): pl.pallas_call(hand_on, out_shape=[jax.ShapeDtypeStruct(block, F32)] * 2,...]
where the time goes in v2:
time: 109 us
  Pallas kernels  107 us (98%)
  between operations  2.09 us (2%)
    pallas_call x1, Pallas kernels, shards(): pl.pallas_call(body, out_shape=[jax.ShapeDtypeStruct(block, F32)] * 2, in...  105 us
    pallas_call x1, Pallas kernels, shards(): pl.pallas_call(hand_on, out_shape=[jax.ShapeDtypeStruct(block, F32)] * 2,...  2.39 us

profile of v2, /device:TPU:1, one launch (start us, length us, event | category | flops | bytes accessed | tf_op | source)
XLA Modules:
  0.0 109.1 jit_solution(37932376690400246)
XLA Ops:
  1.9 104.6 %shard_map.95 = (f32[16,128,128]{2,1,0:T(8,128)}, f32[16,128,128]{2,1,0:T(8,128)}) custom-call(f32[1]{0:T(128)S(6)} %copy.10.refs_0_, f32[1]{0:T(128)S(6)} %copy.11.refs_1_, f32[16,128,128]{2,1,0:T(8,128)} %bitcast.10, f32[16,128,128]{2,1,0:T(8,128)} %bitcast.11, f32[128,128]{1,0:T(8,128)} %bitcast.15, f32[27,18,4,128]{3,2,1,0:T(4,128)} %bitcast.14, ...), custom_call_target="tpu_custom_call" | custom-call | flops 60000002048 | bytes 8388608 | tf_op jit(solution)/shard_map/pallas_call | solution.py:420
  106.5 2.4 %shard_map.96 = (f32[16,128,128]{2,1,0:T(8,128)}, f32[16,128,128]{2,1,0:T(8,128)}) custom-call(f32[16,128,128]{2,1,0:T(8,128)} %get-tuple-element.6.first_in, f32[16,128,128]{2,1,0:T(8,128)} %get-tuple-element.7.second_in), custom_call_target="tpu_custom_call" | custom-call | bytes 4194304 | tf_op jit(solution)/shard_map/pallas_call | solution.py:462

commit v3 on v2

--- a/solution.py
+++ b/solution.py
@@ -377,7 +377,7 @@
         for band in range(BANDS):
             stencil(band)
 
-        scatter(first, 0, result, 1, lambda: couple(second, 1))
+        scatter(first, 0, result, 0, lambda: couple(second, 1))
         scatter(second, 1, result, 0, None)
 
     advance(0, previous, current, following)

time: 109 us -> 105 us (0.963)
  Pallas kernels: 107 us -> 103 us
    pallas_call x1, Pallas kernels: 105 us -> 101 us  [shards(): pl.pallas_call(body, out_shape=[jax.ShapeDtypeStruct(block, F32)] * 2, in...]
where the time goes in v3:
time: 105 us
  Pallas kernels  103 us (98%)
  between operations  2.09 us (2%)
    pallas_call x1, Pallas kernels, shards(): pl.pallas_call(body, out_shape=[jax.ShapeDtypeStruct(block, F32)] * 2, in...  101 us
    pallas_call x1, Pallas kernels, shards(): pl.pallas_call(hand_on, out_shape=[jax.ShapeDtypeStruct(block, F32)] * 2,...  2.39 us

profile of v3, /device:TPU:1, one launch (start us, length us, event | category | flops | bytes accessed | tf_op | source)
XLA Modules:
  0.0 105.2 jit_solution(4962667466293629642)
XLA Ops:
  1.9 100.7 %shard_map.95 = (f32[16,128,128]{2,1,0:T(8,128)}, f32[16,128,128]{2,1,0:T(8,128)}) custom-call(f32[1]{0:T(128)S(6)} %copy.10.refs_0_, f32[1]{0:T(128)S(6)} %copy.11.refs_1_, f32[16,128,128]{2,1,0:T(8,128)} %bitcast.10, f32[16,128,128]{2,1,0:T(8,128)} %bitcast.11, f32[128,128]{1,0:T(8,128)} %bitcast.15, f32[27,18,4,128]{3,2,1,0:T(4,128)} %bitcast.14, ...), custom_call_target="tpu_custom_call" | custom-call | flops 60000002048 | bytes 8388608 | tf_op jit(solution)/shard_map/pallas_call | solution.py:420
  102.7 2.4 %shard_map.96 = (f32[16,128,128]{2,1,0:T(8,128)}, f32[16,128,128]{2,1,0:T(8,128)}) custom-call(f32[16,128,128]{2,1,0:T(8,128)} %get-tuple-element.6.first_in, f32[16,128,128]{2,1,0:T(8,128)} %get-tuple-element.7.second_in), custom_call_target="tpu_custom_call" | custom-call | bytes 4194304 | tf_op jit(solution)/shard_map/pallas_call | solution.py:462
